TPU v7x, 32 devices: a whole 2x2x4 slice. The times are simulated.
32 devices in a mesh: tm: 4 (over z), chan: 8 (over y, x, core).
Axes of the slice: x: 2, y: 2, z: 4, core: 2. Of those that a mesh axis runs over, the one named last changes fastest.
Arguments:
- record: float32 [4096, 1024], P('tm', 'chan'), may hold values from -6 to 6
- fk_mask: int32 [512, 1024], P('chan'), may hold values from 0 to 1, as said below
- tap_table: bfloat16 [8, 8], replicated, may hold values from -0.1875 to 0.1875
- delay_whole: int32 [128, 128], replicated, may hold values from -16 to 16
- tap_index: int32 [128, 128], replicated, may hold values from 0 to 7
Outputs:
- beams: bfloat16 [16, 128, 4096], P('chan', None, 'tm')
Inputs may be any that keep to these rules, and one draw needn't show every extreme that they name: `fk_mask`: 0 or 1; in each row the ones form one contiguous band of signed wavenumbers (k, or k - 1024 for k >= 512) that contains zero.
All inputs are finite; a program needn't handle non-finite values.
Results may differ from a plain program's by a relative error of at most 0.0049.
Values may be sent and summed in bfloat16 or wider, within the bound.
A program may use at most 128 MiB of HBM per device.

v0:
```python
import functools
import math

import jax
import jax.numpy as jnp
import ml_dtypes
import numpy as np
from jax import lax
from jax.experimental import pallas as pl
from jax.experimental.pallas import tpu as pltpu
from jax.sharding import PartitionSpec as P

SUBARRAY = 128
STRIDE = 64
TAPS = 8
FRACS = 8
LAG = 16
RIM = 20
LAGS = 40
GROUPS = 5
SHIFTS = LAGS // GROUPS


def split_table(table):
    high = table.astype(ml_dtypes.bfloat16)
    low = (table - high.astype(np.float64)).astype(ml_dtypes.bfloat16)
    return high, low


def time_table(block_len, devices):
    half_len = block_len // 2
    freq = np.arange(half_len)
    phase = (freq[:, None] * np.arange(block_len)[None, :] % block_len) * (2.0 * math.pi / block_len)
    both = np.stack([np.cos(phase), -np.sin(phase)])
    both = both.reshape(2, devices, half_len // devices, block_len).transpose(1, 0, 2, 3)
    return split_table(both.reshape(block_len, block_len))


def local_table(local_ch):
    ids = np.arange(local_ch)
    phase = (ids[:, None] * ids[None, :] % local_ch) * (2.0 * math.pi / local_ch)
    c, s = np.cos(phase), np.sin(phase)
    return np.block([[c, -s], [s, c]]).astype(np.float32)


def twist_tables(devices, local_ch):
    phase = np.arange(devices)[:, None] * np.arange(local_ch)[None, :] * (2.0 * math.pi / (devices * local_ch))
    return np.cos(phase).astype(np.float32), np.sin(phase).astype(np.float32)


def small_dft(re, im, sign):
    count = len(re)
    if count == 1:
        return re, im
    even_re, even_im = small_dft(re[0::2], im[0::2], sign)
    odd_re, odd_im = small_dft(re[1::2], im[1::2], sign)
    out_re, out_im = [None] * count, [None] * count
    half = count // 2
    for k in range(half):
        if k == 0:
            tr, ti = odd_re[k], odd_im[k]
        elif 4 * k == count:
            tr, ti = -sign * odd_im[k], sign * odd_re[k]
        else:
            c = math.cos(2.0 * math.pi * k / count)
            s = sign * math.sin(2.0 * math.pi * k / count)
            tr = odd_re[k] * c - odd_im[k] * s
            ti = odd_im[k] * c + odd_re[k] * s
        out_re[k], out_im[k] = even_re[k] + tr, even_im[k] + ti
        out_re[k + half], out_im[k + half] = even_re[k] - tr, even_im[k] - ti
    return out_re, out_im


def flip_wavenumbers(rows_table):
    return jnp.roll(rows_table[:, ::-1], 1, axis=1)


def grouped_weights(tap_table, delay_whole, tap_index):
    table = tap_table.astype(jnp.float32)
    coeffs = []
    for tap_pos in range(TAPS):
        value = jnp.zeros(tap_index.shape, jnp.float32)
        for frac in range(FRACS):
            value = jnp.where(tap_index == frac, table[frac, tap_pos], value)
        coeffs.append(value)
    lag = (
        SHIFTS * jnp.arange(GROUPS, dtype=jnp.int32)[:, None, None, None]
        + jnp.arange(SHIFTS, dtype=jnp.int32)[None, None, :, None]
    )
    tap = lag - (delay_whole + LAG)[None, :, None, :]
    weights = jnp.zeros(tap.shape, jnp.float32)
    for tap_pos in range(TAPS):
        weights = jnp.where(tap == tap_pos, coeffs[tap_pos][None, :, None, :], weights)
    rows = GROUPS * delay_whole.shape[0]
    return weights.astype(jnp.bfloat16).reshape(rows, SHIFTS * delay_whole.shape[1])


def dot_f32(left_op, right_op, precision=None):
    return jnp.dot(left_op, right_op, precision=precision, preferred_element_type=jnp.float32)


def body(record, fk_mask, tap_table, delay_whole, tap_index):
    block_len, local_ch = record.shape
    devices = lax.axis_size("chan")
    band_rows, channels = fk_mask.shape
    slow_count = delay_whole.shape[0]
    table_hi, table_lo = time_table(block_len, devices)
    table_hi, table_lo = jnp.asarray(table_hi), jnp.asarray(table_lo)

    rec_hi = record.astype(jnp.bfloat16)
    rec_lo = (record - rec_hi.astype(jnp.float32)).astype(jnp.bfloat16)
    first = dot_f32(table_hi, jnp.concatenate([rec_hi, rec_lo], axis=1))
    spectrum = first[:, :local_ch] + first[:, local_ch:] + dot_f32(table_lo, rec_hi)
    sent = spectrum.astype(jnp.bfloat16).reshape(devices, 2 * band_rows, local_ch)
    got = lax.all_to_all(sent, "chan", split_axis=0, concat_axis=0, tiled=True)

    own_band = fk_mask.astype(jnp.float32)
    freq = lax.axis_index("chan") * band_rows + jnp.arange(band_rows, dtype=jnp.int32)
    at_zero = (freq == 0)[:, None]
    band = jnp.where(at_zero, own_band * flip_wavenumbers(own_band), own_band)
    scale = jnp.where(at_zero, 1.0, 2.0) / (block_len * channels)
    band = (band * scale).reshape(band_rows, local_ch, devices).transpose(2, 0, 1)
    band = band.reshape(devices * band_rows, local_ch)

    cos_twist, sin_twist = twist_tables(devices, local_ch)
    mix = local_table(local_ch)
    parts = got.astype(jnp.float32)
    re, im = small_dft(
        [parts[d, :band_rows] for d in range(devices)],
        [parts[d, band_rows:] for d in range(devices)],
        -1.0,
    )
    turned = []
    for d in range(devices):
        c, s = cos_twist[d][None], sin_twist[d][None]
        turned.append(jnp.concatenate([re[d] * c + im[d] * s, im[d] * c - re[d] * s], axis=1))
    wave = dot_f32(jnp.concatenate(turned, axis=0), mix, lax.Precision.HIGH)
    kept = wave * jnp.concatenate([band, band], axis=1)
    back = dot_f32(kept, mix.T, lax.Precision.HIGH).reshape(devices, band_rows, 2 * local_ch)
    re, im = [], []
    for d in range(devices):
        c, s = cos_twist[d][None], sin_twist[d][None]
        b_re, b_im = back[d, :, :local_ch], back[d, :, local_ch:]
        re.append(b_re * c - b_im * s)
        im.append(b_im * c + b_re * s)
    re, im = small_dft(re, im, 1.0)
    reach = SUBARRAY - STRIDE
    slabs = []
    for d in range(devices):
        if d + 1 < devices:
            rim = jnp.concatenate([re[d + 1][:, :reach], im[d + 1][:, :reach]], axis=1)
        else:
            rim = jnp.zeros((band_rows, 2 * reach), jnp.float32)
        slabs.append(jnp.concatenate([re[d], im[d], rim], axis=0).astype(jnp.bfloat16))
    back_got = lax.all_to_all(jnp.stack(slabs), "chan", split_axis=0, concat_axis=0, tiled=True)
    own = back_got[:, : 2 * band_rows].reshape(block_len, local_ch)
    rim = back_got[:, 2 * band_rows :].reshape(devices, band_rows, 2, reach)
    rim = rim.transpose(0, 2, 1, 3).reshape(block_len, reach)
    rows = jnp.concatenate([own, rim], axis=1)
    contract = (((0,), (0,)), ((), ()))
    field = lax.dot_general(rows, table_hi, contract, preferred_element_type=jnp.float32)
    field = field + lax.dot_general(rows, table_lo, contract, preferred_element_type=jnp.float32)
    filtered = field.astype(jnp.bfloat16)

    count = lax.axis_size("tm")
    forward = [(i, i + 1) for i in range(count - 1)]
    backward = [(i + 1, i) for i in range(count - 1)]
    low = lax.ppermute(filtered[:, block_len - RIM :], "tm", forward)
    high = lax.ppermute(filtered[:, :RIM], "tm", backward)
    extended = jnp.concatenate([low, filtered, high], axis=1)

    weights = grouped_weights(tap_table, delay_whole, tap_index)
    span = block_len + SHIFTS * (GROUPS - 1)
    shifted = jnp.stack([extended[:, r + 1 : r + 1 + span] for r in range(SHIFTS)])
    beams = []
    for a in range(local_ch // STRIDE):
        chosen = shifted[:, a * STRIDE : a * STRIDE + SUBARRAY].reshape(SHIFTS * SUBARRAY, span)
        sums = dot_f32(weights, chosen).reshape(GROUPS, slow_count, span)
        total = sums[0, :, :block_len]
        for g in range(1, GROUPS):
            total = total + sums[g, :, SHIFTS * g : SHIFTS * g + block_len]
        beams.append(total)
    return jnp.stack(beams).astype(jnp.bfloat16)


TILE = 128
EXTRA = 128
MESH = pl.DeviceIdType.MESH


def flipped_bits(number, mask, count):
    result, bit = 0, 1
    while bit < count:
        digit = number // bit % 2
        result = result + (1 - digit if mask // bit % 2 else digit) * bit
        bit *= 2
    return result


def triple(table):
    high, low = split_table(table.astype(np.float64))
    return np.concatenate([high, high, low], axis=0)


def split_dot(left_op, right_ref):
    high = left_op.astype(jnp.bfloat16)
    low = (left_op - high.astype(jnp.float32)).astype(jnp.bfloat16)
    return dot_f32(jnp.concatenate([high, low, high], axis=1), right_ref[...])


def fused(
    devices,
    blocks,
    tap_ref,
    rec_hbm,
    mask_hbm,
    delay_hbm,
    index_hbm,
    mix_hbm,
    unmix_hbm,
    cos_hbm,
    sin_hbm,
    high_hbm,
    low_hbm,
    out_ref,
    rec_ref,
    mask_ref,
    delay_ref,
    index_ref,
    mix_ref,
    unmix_ref,
    cos_ref,
    sin_ref,
    high,
    low,
    rec_pair,
    sent,
    got,
    wave,
    band,
    back_sent,
    back_got,
    rows_t,
    ext,
    weights,
    shifted,
    sums,
    load_sem,
    table_sem,
    send_sem,
    recv_sem,
    halo_send,
    halo_recv,
):
    me = lax.axis_index("chan")
    blk = lax.axis_index("tm")
    block_len, local_ch = rec_ref.shape
    band_rows, channels = mask_ref.shape
    slow_count = delay_ref.shape[0]
    reach = SUBARRAY - STRIDE
    slab = 2 * band_rows
    has_low = jnp.where(blk > 0, 1, 0)
    has_high = jnp.where(blk < blocks - 1, 1, 0)
    order = list(range(devices - 1, 0, -1)) + [0]
    peer = {k: flipped_bits(me, k, devices) for k in order}

    loads = [
        pltpu.make_async_copy(source, target, load_sem.at[place])
        for place, (source, target) in enumerate(
            (
                (rec_hbm, rec_ref),
                (mask_hbm, mask_ref),
                (delay_hbm, delay_ref),
                (index_hbm, index_ref),
                (mix_hbm, mix_ref),
                (unmix_hbm, unmix_ref),
                (cos_hbm, cos_ref),
                (sin_hbm, sin_ref),
            )
        )
    ]
    loads[0].start()
    table_copies = {}
    for k in order:
        rows = pl.ds(pl.multiple_of(peer[k] * slab, slab), slab)
        table_copies[k] = (
            pltpu.make_async_copy(high_hbm.at[rows], high.at[rows], table_sem.at[0, k]),
            pltpu.make_async_copy(low_hbm.at[rows], low.at[rows], table_sem.at[1, k]),
        )
        for copy in table_copies[k]:
            copy.start()

    for load in loads[1:]:
        load.start()

    barrier = pltpu.get_barrier_semaphore()
    for k in order[:-1]:
        pl.semaphore_signal(barrier, inc=1, device_id=(blk, peer[k]), device_id_type=MESH)

    @pl.when(blk > 0)
    def _():
        pl.semaphore_signal(barrier, inc=1, device_id=(blk - 1, me), device_id_type=MESH)

    @pl.when(blk < blocks - 1)
    def _():
        pl.semaphore_signal(barrier, inc=1, device_id=(blk + 1, me), device_id_type=MESH)

    loads[0].wait()
    record = rec_ref[...]
    rec_high = record.astype(jnp.bfloat16)
    rec_pair[:, :local_ch] = rec_high
    rec_pair[:, local_ch:] = (record - rec_high.astype(jnp.float32)).astype(jnp.bfloat16)
    pl.semaphore_wait(barrier, devices - 1 + has_low + has_high)

    copies = {}
    for k in order:
        for copy in table_copies[k]:
            copy.wait()
        rows = pl.ds(pl.multiple_of(peer[k] * slab, slab), slab)
        first = dot_f32(high[rows, :], rec_pair[...])
        part = first[:, :local_ch] + first[:, local_ch:]
        part = part + dot_f32(low[rows, :], rec_pair[:, :local_ch])
        if k == 0:
            got[me] = part.astype(jnp.bfloat16)
        else:
            sent[k] = part.astype(jnp.bfloat16)
            copies[k] = pltpu.make_async_remote_copy(
                src_ref=sent.at[k],
                dst_ref=got.at[me],
                send_sem=send_sem.at[0, k],
                recv_sem=recv_sem.at[0, k],
                device_id=(blk, peer[k]),
                device_id_type=MESH,
            )
            copies[k].start()

    for load in loads[1:]:
        load.wait()
    mask = mask_ref[...].astype(jnp.float32).astype(jnp.bfloat16)
    wave_id = lax.broadcasted_iota(jnp.int32, (channels, local_ch), 0)
    lane_id = lax.broadcasted_iota(jnp.int32, (channels, local_ch), 1)
    bands = []
    for k1 in range(devices):
        pick = jnp.where(wave_id == lane_id * devices + k1, 1.0, 0.0).astype(jnp.bfloat16)
        bands.append(dot_f32(mask, pick))
    from_id = lax.broadcasted_iota(jnp.int32, (local_ch, local_ch), 0)
    to_id = lax.broadcasted_iota(jnp.int32, (local_ch, local_ch), 1)
    freq = lax.broadcasted_iota(jnp.int32, (band_rows, local_ch), 0) + me * band_rows
    scale = jnp.where(freq == 0, 1.0, 2.0) / (block_len * channels)
    for k1 in range(devices):
        total = from_id + to_id
        if k1 == 0:
            turn = jnp.where((total == local_ch) | (total == 0), 1.0, 0.0)
        else:
            turn = jnp.where(total == local_ch - 1, 1.0, 0.0)
        mirror = dot_f32(bands[(devices - k1) % devices].astype(jnp.bfloat16), turn.astype(jnp.bfloat16))
        own = jnp.where(freq == 0, bands[k1] * mirror, bands[k1]) * scale
        band[k1 * band_rows : (k1 + 1) * band_rows] = own

    table = tap_ref[...].astype(jnp.float32)
    for half in range(0, slow_count, 32):
        some = slice(half, half + 32)
        start = delay_ref[some] + LAG
        index = index_ref[some]
        coeffs = []
        for tap_pos in range(TAPS):
            value = jnp.zeros(index.shape, jnp.float32)
            for frac in range(FRACS):
                value = jnp.where(index == frac, table[frac : frac + 1, tap_pos : tap_pos + 1], value)
            coeffs.append(value)
        for lag in range(LAGS):
            value = jnp.zeros(index.shape, jnp.float32)
            for tap_pos in range(TAPS):
                value = jnp.where(start == lag - tap_pos, coeffs[tap_pos], value)
            g, r = divmod(lag, SHIFTS)
            weights[
                g * slow_count + half : g * slow_count + half + 32, r * SUBARRAY : (r + 1) * SUBARRAY
            ] = value.astype(jnp.bfloat16)

    for k in order[:-1]:
        copies[k].wait_recv()

    step = 16
    for low_row in range(0, band_rows, step):
        re = [got[d, low_row : low_row + step].astype(jnp.float32) for d in range(devices)]
        im = [
            got[d, band_rows + low_row : band_rows + low_row + step].astype(jnp.float32)
            for d in range(devices)
        ]
        re, im = small_dft(re, im, -1.0)
        for d in range(devices):
            c, s = cos_ref[d : d + 1], sin_ref[d : d + 1]
            rows = slice(d * band_rows + low_row, d * band_rows + low_row + step)
            wave[rows, :local_ch] = re[d] * c + im[d] * s
            wave[rows, local_ch:] = im[d] * c - re[d] * s
    spread = split_dot(wave[...], mix_ref)
    kept = spread * jnp.concatenate([band[...], band[...]], axis=1)
    wave[...] = split_dot(kept, unmix_ref)
    for low_row in range(0, band_rows, step):
        re, im = [], []
        for d in range(devices):
            c, s = cos_ref[d : d + 1], sin_ref[d : d + 1]
            rows = slice(d * band_rows + low_row, d * band_rows + low_row + step)
            b_re, b_im = wave[rows, :local_ch], wave[rows, local_ch:]
            re.append(b_re * c - b_im * s)
            im.append(b_im * c + b_re * s)
        re, im = small_dft(re, im, 1.0)
        for d in range(devices):
            if d + 1 < devices:
                rim = jnp.concatenate([re[d + 1][:, :reach], im[d + 1][:, :reach]], axis=1)
            else:
                rim = jnp.zeros((step, 2 * reach), jnp.float32)
            for place, part in enumerate((re[d], im[d], rim)):
                rows = slice(place * band_rows + low_row, place * band_rows + low_row + step)
                back_sent[d, rows] = part.astype(jnp.bfloat16)

    back_copies = {}
    for k in order[:-1]:
        back_copies[k] = pltpu.make_async_remote_copy(
            src_ref=back_sent.at[peer[k]],
            dst_ref=back_got.at[me],
            send_sem=send_sem.at[1, k],
            recv_sem=recv_sem.at[1, k],
            device_id=(blk, peer[k]),
            device_id_type=MESH,
        )
        back_copies[k].start()
    back_got[me] = back_sent[me]
    for k in order[::-1]:
        if k:
            back_copies[k].wait_recv()
        source = peer[k]
        piece = back_got[source].astype(jnp.float32)
        lanes = pl.ds(pl.multiple_of(source * slab, slab), slab)
        rows_t[:local_ch, lanes] = piece[:slab].T.astype(jnp.bfloat16)
        rim = piece[slab:].T
        rim = jnp.concatenate([rim[:reach], rim[reach:]], axis=1)
        rows_t[local_ch:, lanes] = rim.astype(jnp.bfloat16)

    def back_in_time(first, width):
        left_op = rows_t[...]
        field = dot_f32(left_op, high[:, first : first + width])
        field = field + dot_f32(left_op, low[:, first : first + width])
        ext[:, EXTRA + first : EXTRA + first + width] = field.astype(jnp.bfloat16)

    chunk = 2 * TILE
    back_in_time(0, chunk)
    back_in_time(block_len - chunk, chunk)
    last = EXTRA + block_len
    up = pltpu.make_async_remote_copy(
        src_ref=ext.at[:, block_len:last],
        dst_ref=ext.at[:, 0:EXTRA],
        send_sem=halo_send.at[0],
        recv_sem=halo_recv.at[0],
        device_id=(blk + 1, me),
        device_id_type=MESH,
    )
    down = pltpu.make_async_remote_copy(
        src_ref=ext.at[:, EXTRA : 2 * EXTRA],
        dst_ref=ext.at[:, last : last + EXTRA],
        send_sem=halo_send.at[1],
        recv_sem=halo_recv.at[1],
        device_id=(blk - 1, me),
        device_id_type=MESH,
    )

    @pl.when(blk < blocks - 1)
    def _():
        up.start()

    @pl.when(blk > 0)
    def _():
        down.start()

    for first in range(chunk, block_len - chunk, chunk):
        back_in_time(first, chunk)

    @pl.when(blk > 0)
    def _():
        up.wait_recv()

    @pl.when(blk == 0)
    def _():
        ext[:, 0:EXTRA] = jnp.zeros((ext.shape[0], EXTRA), jnp.bfloat16)

    @pl.when(blk < blocks - 1)
    def _():
        down.wait_recv()

    @pl.when(blk == blocks - 1)
    def _():
        ext[:, last : last + EXTRA] = jnp.zeros((ext.shape[0], EXTRA), jnp.bfloat16)

    span = block_len + EXTRA
    for r in range(SHIFTS):
        begin = EXTRA - RIM + 1 + r
        moved = ext[:, begin : begin + span]
        rows = slice(r * SUBARRAY, (r + 1) * SUBARRAY)
        for a in range(local_ch // STRIDE):
            shifted[rows, a * span : (a + 1) * span] = moved[a * STRIDE : a * STRIDE + SUBARRAY]

    @pl.loop(0, shifted.shape[1] // chunk)
    def _(n):
        lanes = pl.ds(pl.multiple_of(n * chunk, chunk), chunk)
        sums[:, lanes] = dot_f32(weights[...], shifted[:, lanes])

    @pl.loop(0, slow_count // step)
    def _(n):
        for a in range(local_ch // STRIDE):
            total = None
            for g in range(GROUPS):
                rows = pl.ds(pl.multiple_of(g * slow_count + n * step, step), step)
                begin = a * span + SHIFTS * g
                part = sums[rows, a * span : (a + 1) * span][:, SHIFTS * g : SHIFTS * g + block_len]
                total = part if total is None else total + part
            out_ref[a, pl.ds(pl.multiple_of(n * step, step), step), :] = total.astype(jnp.bfloat16)

    for k in order[:-1]:
        copies[k].wait_send()
        back_copies[k].wait_send()

    @pl.when(blk < blocks - 1)
    def _():
        up.wait_send()

    @pl.when(blk > 0)
    def _():
        down.wait_send()


def fused_body(devices, blocks, record, fk_mask, tap_table, delay_whole, tap_index):
    block_len, local_ch = record.shape
    band_rows, channels = fk_mask.shape
    slow_count = delay_whole.shape[0]
    table_hi, table_lo = time_table(block_len, devices)
    cos_twist, sin_twist = twist_tables(devices, local_ch)
    mix = local_table(local_ch)
    slab = 2 * band_rows
    reach = SUBARRAY - STRIDE
    span = block_len + EXTRA
    subarrays = local_ch // STRIDE
    bf16 = jnp.bfloat16
    vmem = pl.BlockSpec(memory_space=pltpu.VMEM)
    hbm = pl.BlockSpec(memory_space=pltpu.HBM)
    return pl.pallas_call(
        functools.partial(fused, devices, blocks),
        out_shape=jax.ShapeDtypeStruct((subarrays, slow_count, block_len), bf16),
        in_specs=[vmem] + [hbm] * 10,
        out_specs=vmem,
        scratch_shapes=[
            pltpu.VMEM((block_len, local_ch), jnp.float32),
            pltpu.VMEM((band_rows, channels), jnp.int32),
            pltpu.VMEM((slow_count, SUBARRAY), jnp.int32),
            pltpu.VMEM((slow_count, SUBARRAY), jnp.int32),
            pltpu.VMEM((6 * local_ch, 2 * local_ch), bf16),
            pltpu.VMEM((6 * local_ch, 2 * local_ch), bf16),
            pltpu.VMEM((devices, local_ch), jnp.float32),
            pltpu.VMEM((devices, local_ch), jnp.float32),
            pltpu.VMEM((block_len, block_len), bf16),
            pltpu.VMEM((block_len, block_len), bf16),
            pltpu.VMEM((block_len, 2 * local_ch), bf16),
            pltpu.VMEM((devices, slab, local_ch), bf16),
            pltpu.VMEM((devices, slab, local_ch), bf16),
            pltpu.VMEM((devices * band_rows, 2 * local_ch), jnp.float32),
            pltpu.VMEM((devices * band_rows, local_ch), jnp.float32),
            pltpu.VMEM((devices, slab + band_rows, local_ch), bf16),
            pltpu.VMEM((devices, slab + band_rows, local_ch), bf16),
            pltpu.VMEM((local_ch + reach, block_len), bf16),
            pltpu.VMEM((local_ch + reach, block_len + 2 * EXTRA), bf16),
            pltpu.VMEM((GROUPS * slow_count, SHIFTS * SUBARRAY), bf16),
            pltpu.VMEM((SHIFTS * SUBARRAY, subarrays * span), bf16),
            pltpu.VMEM((GROUPS * slow_count, subarrays * span), jnp.float32),
            pltpu.SemaphoreType.DMA((8,)),
            pltpu.SemaphoreType.DMA((2, devices)),
            pltpu.SemaphoreType.DMA((2, devices)),
            pltpu.SemaphoreType.DMA((2, devices)),
            pltpu.SemaphoreType.DMA((2,)),
            pltpu.SemaphoreType.DMA((2,)),
        ],
        compiler_params=pltpu.CompilerParams(
            collective_id=0, has_side_effects=True, vmem_limit_bytes=63 * 2**20
        ),
    )(
        tap_table,
        record,
        fk_mask,
        delay_whole,
        tap_index,
        jnp.asarray(triple(mix)),
        jnp.asarray(triple(mix.T)),
        jnp.asarray(cos_twist),
        jnp.asarray(sin_twist),
        jnp.asarray(table_hi),
        jnp.asarray(table_lo),
    )


def solution(mesh):
    placed = (P("tm", "chan"), P("chan", None), P(), P(), P())
    devices, blocks = mesh.shape["chan"], mesh.shape["tm"]

    def placed_body(record, *others):
        block_len, local_ch = record.shape
        if local_ch == TILE and block_len // devices == TILE:
            return fused_body(devices, blocks, record, *others)
        return body(record, *others)

    return jax.shard_map(
        placed_body, mesh=mesh, in_specs=placed, out_specs=P("chan", None, "tm"), check_vma=False
    )
```

profile of v0, /device:TPU:0, one launch (start us, length us, event | category | flops | bytes accessed | tf_op | source)
XLA Modules:
  0.0 32.9 jit_solution(3776064411594569714)
XLA Ops:
  0.0 31.0 %shard_map.109 = bf16[2,128,1024]{2,1,0:T(8,128)(2,1)} custom-call(bf16[8,8]{1,0:T(8,128)(2,1)} %tap_ref.1, f32[1024,128]{1,0:T(8,128)} %rec_hbm.1, s32[64,1024]{1,0:T(8,128)} %mask_hbm.1, s32[128,128]{1,0:T(8,128)} %delay_hbm.1, s32[128,128]{1,0:T(8,128)} %index_hbm.1, bf16[768,256]{1,0:T(8,128)(2,1)} %constant.12.clone.mix_hbm, ...), custom_call_target="tpu_custom_call" | custom-call | tf_op jit(solution)/shard_map/pallas_call | solution.py:545
  31.0 1.9 %copy.13 = bf16[2,128,1024]{2,1,0:T(8,128)(2,1)} copy(bf16[2,128,1024]{2,1,0:T(8,128)(2,1)} %shard_map.109) | data formatting | bytes 1048576
where the time goes:
time: 33.1 us; the launch traced here: 32.9 us
  Pallas kernels  31 us (94%)
  local copies, waits for them, and re-layouts  1.87 us (6%)
    pallas_call x1, Pallas kernels, fused_body(): pl.pallas_call(functools.partial(fused, devices, blocks), out_shape=jax.S...  31 us
    unnamed x1, local copies, waits for them, and re-layouts  1.87 us

commit v1 on v0

--- a/solution.py
+++ b/solution.py
@@ -544,7 +544,7 @@
     hbm = pl.BlockSpec(memory_space=pltpu.HBM)
     return pl.pallas_call(
         functools.partial(fused, devices, blocks),
-        out_shape=jax.ShapeDtypeStruct((subarrays, slow_count, block_len), bf16),
+        out_shape=pltpu.VMEM((subarrays, slow_count, block_len), bf16),
         in_specs=[vmem] + [hbm] * 10,
         out_specs=vmem,
         scratch_shapes=[
@@ -578,7 +578,7 @@
             pltpu.SemaphoreType.DMA((2,)),
         ],
         compiler_params=pltpu.CompilerParams(
-            collective_id=0, has_side_effects=True, vmem_limit_bytes=63 * 2**20
+            collective_id=0, has_side_effects=True, vmem_limit_bytes=60 * 2**20
         ),
     )(
         tap_table,

time: 33.1 us -> 31.2 us (0.943)
  local copies, waits for them, and re-layouts: 1.87 us -> 0.8 us
  Pallas kernels: 31 us -> 30.2 us
    unnamed x1, local copies, waits for them, and re-layouts: 1.87 us -> 0.8 us
    pallas_call x1, Pallas kernels: 31 us -> 30.2 us  [fused_body(): pl.pallas_call(functools.partial(fused, devices, blocks), out_shape=pltpu...]
where the time goes in v1:
time: 31.2 us; the launch traced here: 31.1 us
  Pallas kernels  30.2 us (97%)
  local copies, waits for them, and re-layouts  0.8 us (3%)
    pallas_call x1, Pallas kernels, fused_body(): pl.pallas_call(functools.partial(fused, devices, blocks), out_shape=pltpu...  30.2 us
    unnamed x1, local copies, waits for them, and re-layouts  0.8 us

profile of v1, /device:TPU:0, one launch (start us, length us, event | category | flops | bytes accessed | tf_op | source)
XLA Modules:
  0.0 31.1 jit_solution(5379739931361563393)
XLA Ops:
  0.0 30.2 %shard_map.109 = bf16[2,128,1024]{2,1,0:T(8,128)(2,1)S(1)} custom-call(bf16[8,8]{1,0:T(8,128)(2,1)} %tap_ref.1, f32[1024,128]{1,0:T(8,128)} %rec_hbm.1, s32[64,1024]{1,0:T(8,128)} %mask_hbm.1, s32[128,128]{1,0:T(8,128)} %delay_hbm.1, s32[128,128]{1,0:T(8,128)} %index_hbm.1, bf16[768,256]{1,0:T(8,128)(2,1)} %constant.12.clone.mix_hbm, ...), custom_call_target="tpu_custom_call" | custom-call | tf_op jit(solution)/shard_map/pallas_call | solution.py:545
  30.3 0.8 %copy.13 = bf16[2,128,1024]{2,1,0:T(8,128)(2,1)} copy(bf16[2,128,1024]{2,1,0:T(8,128)(2,1)S(1)} %shard_map.109) | data formatting | bytes 1048576

commit v2 on v1

v2 whole, which is shorter than its diff:
```python
import functools
import math

import jax
import jax.numpy as jnp
import ml_dtypes
import numpy as np
from jax import lax
from jax.experimental import pallas as pl
from jax.experimental.pallas import tpu as pltpu
from jax.sharding import PartitionSpec as P

SUBARRAY = 128
STRIDE = 64
TAPS = 8
FRACS = 8
LAG = 16
RIM = 20
LAGS = 40
GROUPS = 5
SHIFTS = LAGS // GROUPS


def split_table(table):
    high = table.astype(ml_dtypes.bfloat16)
    low = (table - high.astype(np.float64)).astype(ml_dtypes.bfloat16)
    return high, low


def time_table(block_len, devices):
    half_len = block_len // 2
    freq = np.arange(half_len)
    phase = (freq[:, None] * np.arange(block_len)[None, :] % block_len) * (2.0 * math.pi / block_len)
    both = np.stack([np.cos(phase), -np.sin(phase)])
    both = both.reshape(2, devices, half_len // devices, block_len).transpose(1, 0, 2, 3)
    return split_table(both.reshape(block_len, block_len))


def local_table(local_ch):
    ids = np.arange(local_ch)
    phase = (ids[:, None] * ids[None, :] % local_ch) * (2.0 * math.pi / local_ch)
    c, s = np.cos(phase), np.sin(phase)
    return np.block([[c, -s], [s, c]]).astype(np.float32)


def twist_tables(devices, local_ch):
    phase = np.arange(devices)[:, None] * np.arange(local_ch)[None, :] * (2.0 * math.pi / (devices * local_ch))
    return np.cos(phase).astype(np.float32), np.sin(phase).astype(np.float32)


def small_dft(re, im, sign):
    count = len(re)
    if count == 1:
        return re, im
    even_re, even_im = small_dft(re[0::2], im[0::2], sign)
    odd_re, odd_im = small_dft(re[1::2], im[1::2], sign)
    out_re, out_im = [None] * count, [None] * count
    half = count // 2
    for k in range(half):
        if k == 0:
            tr, ti = odd_re[k], odd_im[k]
        elif 4 * k == count:
            tr, ti = -sign * odd_im[k], sign * odd_re[k]
        else:
            c = math.cos(2.0 * math.pi * k / count)
            s = sign * math.sin(2.0 * math.pi * k / count)
            tr = odd_re[k] * c - odd_im[k] * s
            ti = odd_im[k] * c + odd_re[k] * s
        out_re[k], out_im[k] = even_re[k] + tr, even_im[k] + ti
        out_re[k + half], out_im[k + half] = even_re[k] - tr, even_im[k] - ti
    return out_re, out_im


def flip_wavenumbers(rows_table):
    return jnp.roll(rows_table[:, ::-1], 1, axis=1)


def grouped_weights(tap_table, delay_whole, tap_index):
    table = tap_table.astype(jnp.float32)
    coeffs = []
    for tap_pos in range(TAPS):
        value = jnp.zeros(tap_index.shape, jnp.float32)
        for frac in range(FRACS):
            value = jnp.where(tap_index == frac, table[frac, tap_pos], value)
        coeffs.append(value)
    lag = (
        SHIFTS * jnp.arange(GROUPS, dtype=jnp.int32)[:, None, None, None]
        + jnp.arange(SHIFTS, dtype=jnp.int32)[None, None, :, None]
    )
    tap = lag - (delay_whole + LAG)[None, :, None, :]
    weights = jnp.zeros(tap.shape, jnp.float32)
    for tap_pos in range(TAPS):
        weights = jnp.where(tap == tap_pos, coeffs[tap_pos][None, :, None, :], weights)
    rows = GROUPS * delay_whole.shape[0]
    return weights.astype(jnp.bfloat16).reshape(rows, SHIFTS * delay_whole.shape[1])


def dot_f32(left_op, right_op, precision=None):
    return jnp.dot(left_op, right_op, precision=precision, preferred_element_type=jnp.float32)


def body(record, fk_mask, tap_table, delay_whole, tap_index):
    block_len, local_ch = record.shape
    devices = lax.axis_size("chan")
    band_rows, channels = fk_mask.shape
    slow_count = delay_whole.shape[0]
    table_hi, table_lo = time_table(block_len, devices)
    table_hi, table_lo = jnp.asarray(table_hi), jnp.asarray(table_lo)

    rec_hi = record.astype(jnp.bfloat16)
    rec_lo = (record - rec_hi.astype(jnp.float32)).astype(jnp.bfloat16)
    first = dot_f32(table_hi, jnp.concatenate([rec_hi, rec_lo], axis=1))
    spectrum = first[:, :local_ch] + first[:, local_ch:] + dot_f32(table_lo, rec_hi)
    sent = spectrum.astype(jnp.bfloat16).reshape(devices, 2 * band_rows, local_ch)
    got = lax.all_to_all(sent, "chan", split_axis=0, concat_axis=0, tiled=True)

    own_band = fk_mask.astype(jnp.float32)
    freq = lax.axis_index("chan") * band_rows + jnp.arange(band_rows, dtype=jnp.int32)
    at_zero = (freq == 0)[:, None]
    band = jnp.where(at_zero, own_band * flip_wavenumbers(own_band), own_band)
    scale = jnp.where(at_zero, 1.0, 2.0) / (block_len * channels)
    band = (band * scale).reshape(band_rows, local_ch, devices).transpose(2, 0, 1)
    band = band.reshape(devices * band_rows, local_ch)

    cos_twist, sin_twist = twist_tables(devices, local_ch)
    mix = local_table(local_ch)
    parts = got.astype(jnp.float32)
    re, im = small_dft(
        [parts[d, :band_rows] for d in range(devices)],
        [parts[d, band_rows:] for d in range(devices)],
        -1.0,
    )
    turned = []
    for d in range(devices):
        c, s = cos_twist[d][None], sin_twist[d][None]
        turned.append(jnp.concatenate([re[d] * c + im[d] * s, im[d] * c - re[d] * s], axis=1))
    wave = dot_f32(jnp.concatenate(turned, axis=0), mix, lax.Precision.HIGH)
    kept = wave * jnp.concatenate([band, band], axis=1)
    back = dot_f32(kept, mix.T, lax.Precision.HIGH).reshape(devices, band_rows, 2 * local_ch)
    re, im = [], []
    for d in range(devices):
        c, s = cos_twist[d][None], sin_twist[d][None]
        b_re, b_im = back[d, :, :local_ch], back[d, :, local_ch:]
        re.append(b_re * c - b_im * s)
        im.append(b_im * c + b_re * s)
    re, im = small_dft(re, im, 1.0)
    reach = SUBARRAY - STRIDE
    slabs = []
    for d in range(devices):
        if d + 1 < devices:
            rim = jnp.concatenate([re[d + 1][:, :reach], im[d + 1][:, :reach]], axis=1)
        else:
            rim = jnp.zeros((band_rows, 2 * reach), jnp.float32)
        slabs.append(jnp.concatenate([re[d], im[d], rim], axis=0).astype(jnp.bfloat16))
    back_got = lax.all_to_all(jnp.stack(slabs), "chan", split_axis=0, concat_axis=0, tiled=True)
    own = back_got[:, : 2 * band_rows].reshape(block_len, local_ch)
    rim = back_got[:, 2 * band_rows :].reshape(devices, band_rows, 2, reach)
    rim = rim.transpose(0, 2, 1, 3).reshape(block_len, reach)
    rows = jnp.concatenate([own, rim], axis=1)
    contract = (((0,), (0,)), ((), ()))
    field = lax.dot_general(rows, table_hi, contract, preferred_element_type=jnp.float32)
    field = field + lax.dot_general(rows, table_lo, contract, preferred_element_type=jnp.float32)
    filtered = field.astype(jnp.bfloat16)

    count = lax.axis_size("tm")
    forward = [(i, i + 1) for i in range(count - 1)]
    backward = [(i + 1, i) for i in range(count - 1)]
    low = lax.ppermute(filtered[:, block_len - RIM :], "tm", forward)
    high = lax.ppermute(filtered[:, :RIM], "tm", backward)
    extended = jnp.concatenate([low, filtered, high], axis=1)

    weights = grouped_weights(tap_table, delay_whole, tap_index)
    span = block_len + SHIFTS * (GROUPS - 1)
    shifted = jnp.stack([extended[:, r + 1 : r + 1 + span] for r in range(SHIFTS)])
    beams = []
    for a in range(local_ch // STRIDE):
        chosen = shifted[:, a * STRIDE : a * STRIDE + SUBARRAY].reshape(SHIFTS * SUBARRAY, span)
        sums = dot_f32(weights, chosen).reshape(GROUPS, slow_count, span)
        total = sums[0, :, :block_len]
        for g in range(1, GROUPS):
            total = total + sums[g, :, SHIFTS * g : SHIFTS * g + block_len]
        beams.append(total)
    return jnp.stack(beams).astype(jnp.bfloat16)


TILE = 128
EDGE = 32
PHASE = 8
TURNS = 2 * TILE
MESH = pl.DeviceIdType.MESH


def flipped_bits(number, mask, count):
    result, bit = 0, 1
    while bit < count:
        digit = number // bit % 2
        result = result + (1 - digit if mask // bit % 2 else digit) * bit
        bit *= 2
    return result


def triple(table):
    high, low = split_table(table.astype(np.float64))
    return np.concatenate([high, high, low], axis=0)


def parity_tables(block_len, devices):
    half_len = block_len // 2
    count = half_len // devices // 2
    tables = []
    for parity in range(2):
        freq = np.arange(devices)[:, None] * 2 * count + 2 * np.arange(count)[None, :] + parity
        phase = (freq[:, :, None] * np.arange(half_len) % block_len) * (2.0 * math.pi / block_len)
        tables.append(np.stack([np.cos(phase), -np.sin(phase)], axis=1).reshape(half_len, half_len))
    tables = np.stack(tables)
    ahead = np.concatenate(split_table(tables), axis=2)
    back = np.concatenate(split_table(tables.transpose(0, 2, 1)), axis=2)
    return ahead, back


def split_dot(left_op, right_ref):
    high = left_op.astype(jnp.bfloat16)
    low = (left_op - high.astype(jnp.float32)).astype(jnp.bfloat16)
    return dot_f32(jnp.concatenate([high, low, high], axis=1), right_ref[...])


def fused(
    devices,
    blocks,
    tap_ref,
    rec_hbm,
    mask_hbm,
    delay_hbm,
    index_hbm,
    mix_hbm,
    unmix_hbm,
    cos_hbm,
    sin_hbm,
    ahead_hbm,
    behind_hbm,
    out_ref,
    rec_ref,
    mask_ref,
    delay_ref,
    index_ref,
    mix_ref,
    unmix_ref,
    cos_ref,
    sin_ref,
    ahead,
    behind,
    folded,
    sent,
    got,
    wave,
    band,
    back_sent,
    back_got,
    ext,
    edge_sent,
    edge_got,
    rim_sent,
    rim_got,
    weights,
    shifted,
    load_sem,
    table_sem,
    send_sem,
    recv_sem,
    edge_send,
    edge_recv,
    rim_sem,
):
    me = lax.axis_index("chan")
    blk = lax.axis_index("tm")
    block_len, local_ch = rec_ref.shape
    half_len = block_len // 2
    band_rows, channels = mask_ref.shape
    half_rows = band_rows // 2
    slow_count = delay_ref.shape[0]
    f32, bf16 = jnp.float32, jnp.bfloat16
    is_first, is_last = me == 0, me == devices - 1
    low_blk, high_blk = blk > 0, blk < blocks - 1
    order = list(range(devices - 1, 0, -1))
    peer = {k: flipped_bits(me, k, devices) for k in order}

    def count_of(flag):
        return jnp.where(flag, 1, 0)

    loads = [
        pltpu.make_async_copy(source, target, load_sem.at[place])
        for place, (source, target) in enumerate(
            (
                (rec_hbm, rec_ref),
                (mask_hbm, mask_ref),
                (delay_hbm, delay_ref),
                (index_hbm, index_ref),
                (cos_hbm, cos_ref),
                (sin_hbm, sin_ref),
                (mix_hbm, mix_ref),
                (unmix_hbm, unmix_ref),
            )
        )
    ]
    tables = [
        pltpu.make_async_copy(ahead_hbm.at[0], ahead.at[0], table_sem.at[0]),
        pltpu.make_async_copy(ahead_hbm.at[1], ahead.at[1], table_sem.at[1]),
        pltpu.make_async_copy(behind_hbm, behind, table_sem.at[2]),
    ]
    loads[0].start()
    tables[0].start()

    barrier = pltpu.get_barrier_semaphore()

    def greet(block, shard):
        pl.semaphore_signal(barrier, inc=1, device_id=(block, shard), device_id_type=MESH)

    for k in order:
        greet(blk, peer[k])
    for there, block in ((low_blk, blk - 1), (high_blk, blk + 1)):

        @pl.when(there)
        def _():
            greet(block, me)

        @pl.when(there & (me < devices - 1))
        def _():
            greet(block, me + 1)

    tables[1].start()
    for load in loads[1:]:
        load.start()
    tables[2].start()

    def fold(parity):
        first, second = rec_ref[:half_len], rec_ref[half_len:]
        value = first - second if parity else first + second
        high = value.astype(bf16)
        folded[:half_len, :local_ch] = high
        folded[:half_len, local_ch:] = (value - high.astype(f32)).astype(bf16)
        folded[half_len:, :local_ch] = high
        folded[half_len:, local_ch:] = jnp.zeros_like(high)

    copies = {}
    loads[0].wait()
    for parity in range(2):
        fold(parity)
        tables[parity].wait()
        both = dot_f32(ahead[parity], folded[...])
        part = (both[:, :local_ch] + both[:, local_ch:]).astype(bf16)
        sent[parity] = part.reshape(devices, band_rows, local_ch)
        if parity == 0:
            neighbours = count_of(low_blk) + count_of(high_blk)
            pl.semaphore_wait(barrier, devices - 1 + neighbours * (1 + count_of(me > 0)))
        for k in order:
            copies[parity, k] = pltpu.make_async_remote_copy(
                src_ref=sent.at[parity, peer[k]],
                dst_ref=got.at[parity, me],
                send_sem=send_sem.at[0, parity, k],
                recv_sem=recv_sem.at[0, parity, k],
                device_id=(blk, peer[k]),
                device_id_type=MESH,
            )
            copies[parity, k].start()
        got[parity, me] = sent[parity, me]

    for load in loads[1:]:
        load.wait()
    put_id = lax.broadcasted_iota(jnp.int32, (band_rows, band_rows), 0)
    take_id = lax.broadcasted_iota(jnp.int32, (band_rows, band_rows), 1)
    taken = jnp.where(put_id < half_rows, 2 * put_id, 2 * (put_id - half_rows) + 1)
    sort = jnp.where(take_id == taken, 1.0, 0.0).astype(bf16)
    mask = dot_f32(sort, mask_ref[...].astype(f32).astype(bf16)).astype(bf16)
    wave_id = lax.broadcasted_iota(jnp.int32, (channels, local_ch), 0)
    lane_id = lax.broadcasted_iota(jnp.int32, (channels, local_ch), 1)
    bands = []
    for k1 in range(devices):
        pick = jnp.where(wave_id == lane_id * devices + k1, 1.0, 0.0).astype(bf16)
        bands.append(dot_f32(mask, pick))
    from_id = lax.broadcasted_iota(jnp.int32, (local_ch, local_ch), 0)
    to_id = lax.broadcasted_iota(jnp.int32, (local_ch, local_ch), 1)
    row_id = lax.broadcasted_iota(jnp.int32, (band_rows, local_ch), 0)
    at_zero = (row_id == 0) & is_first
    scale = jnp.where(at_zero, 1.0, 2.0) / (block_len * channels)
    for k1 in range(devices):
        total = from_id + to_id
        if k1 == 0:
            turn = jnp.where((total == local_ch) | (total == 0), 1.0, 0.0)
        else:
            turn = jnp.where(total == local_ch - 1, 1.0, 0.0)
        mirror = dot_f32(bands[(devices - k1) % devices].astype(bf16), turn.astype(bf16))
        own = jnp.where(at_zero, bands[k1] * mirror, bands[k1]) * scale
        for parity in range(2):
            band[parity, k1 * half_rows : (k1 + 1) * half_rows] = own[parity * half_rows : (parity + 1) * half_rows]

    step = 16

    def over_channels(parity):
        for low_row in range(0, half_rows, step):
            re = [got[parity, d, low_row : low_row + step].astype(f32) for d in range(devices)]
            im = [
                got[parity, d, half_rows + low_row : half_rows + low_row + step].astype(f32)
                for d in range(devices)
            ]
            re, im = small_dft(re, im, -1.0)
            for d in range(devices):
                c, s = cos_ref[d : d + 1], sin_ref[d : d + 1]
                rows = slice(d * half_rows + low_row, d * half_rows + low_row + step)
                wave[rows, :local_ch] = re[d] * c + im[d] * s
                wave[rows, local_ch:] = im[d] * c - re[d] * s
        spread = split_dot(wave[...], mix_ref)
        kept = spread * jnp.concatenate([band[parity], band[parity]], axis=1)
        wave[...] = split_dot(kept, unmix_ref)
        for low_row in range(0, half_rows, step):
            re, im = [], []
            for d in range(devices):
                c, s = cos_ref[d : d + 1], sin_ref[d : d + 1]
                rows = slice(d * half_rows + low_row, d * half_rows + low_row + step)
                b_re, b_im = wave[rows, :local_ch], wave[rows, local_ch:]
                re.append(b_re * c - b_im * s)
                im.append(b_im * c + b_re * s)
            re, im = small_dft(re, im, 1.0)
            for d in range(devices):
                back_sent[parity, d, low_row : low_row + step] = re[d].astype(bf16)
                back_sent[parity, d, half_rows + low_row : half_rows + low_row + step] = im[d].astype(bf16)

    back_copies = {}
    for parity in range(2):
        for k in order:
            copies[parity, k].wait_recv()
        over_channels(parity)
        for k in order:
            back_copies[parity, k] = pltpu.make_async_remote_copy(
                src_ref=back_sent.at[parity, peer[k]],
                dst_ref=back_got.at[parity, me],
                send_sem=send_sem.at[1, parity, k],
                recv_sem=recv_sem.at[1, parity, k],
                device_id=(blk, peer[k]),
                device_id_type=MESH,
            )
            back_copies[parity, k].start()
        back_got[parity, me] = back_sent[parity, me]

    tables[2].wait()

    def drain_exchanges():
        for parity in range(2):
            for k in order:
                copies[parity, k].wait_send()
                back_copies[parity, k].wait_send()

    table = tap_ref[...].astype(f32)
    starts = delay_ref[...].astype(f32).T.astype(jnp.int32) + LAG
    index_t = index_ref[...].astype(f32).T.astype(jnp.int32)
    blank = jnp.zeros((PHASE * SUBARRAY, slow_count), bf16)
    weights[LAGS * SUBARRAY :, :slow_count] = blank
    weights[: PHASE * SUBARRAY, slow_count:] = blank
    for first in range(0, SUBARRAY, 32):
        start = starts[first : first + 32]
        index = index_t[first : first + 32]
        coeffs = []
        for tap_pos in range(TAPS):
            value = jnp.zeros(index.shape, f32)
            for frac in range(FRACS):
                value = jnp.where(index == frac, table[frac : frac + 1, tap_pos : tap_pos + 1], value)
            coeffs.append(value)
        for lag in range(LAGS):
            value = jnp.zeros(index.shape, f32)
            for tap_pos in range(TAPS):
                if 0 <= lag - tap_pos <= 2 * LAG:
                    value = jnp.where(start == lag - tap_pos, coeffs[tap_pos], value)
            value = value.astype(bf16)
            for phase in range(2):
                top = (lag + PHASE * phase) * SUBARRAY + first
                weights[top : top + 32, phase * slow_count : (phase + 1) * slow_count] = value
    pieces = []
    for parity in range(2):
        for k in order:
            back_copies[parity, k].wait_recv()
        rows = back_got[parity].reshape(half_len, local_ch)
        pieces.append(dot_f32(behind[parity], jnp.concatenate([rows, rows], axis=0)))
    early, late = pieces[0] + pieces[1], pieces[0] - pieces[1]
    edge_sent[0] = early[:EDGE].astype(bf16)
    edge_sent[1] = late[half_len - EDGE :].astype(bf16)

    def edge_copy(side, beside):
        return pltpu.make_async_remote_copy(
            src_ref=edge_sent.at[side],
            dst_ref=edge_got.at[beside, side],
            send_sem=edge_send.at[beside, side],
            recv_sem=edge_recv.at[beside, side],
            device_id=(blk - 1 + 2 * side, me - beside),
            device_id_type=MESH,
        )

    edges = {(side, beside): edge_copy(side, beside) for side in range(2) for beside in range(2)}
    leaves = (low_blk, high_blk)
    for side in range(2):
        for beside in range(2):

            @pl.when(leaves[side] & (me > 0) if beside else leaves[side])
            def _():
                edges[side, beside].start()

    swapped_early = pltpu.roll(early, STRIDE, 1)
    swapped_late = pltpu.roll(late, STRIDE, 1)
    left = lax.broadcasted_iota(jnp.int32, (half_len, local_ch), 1) < STRIDE
    rim_sent[...] = jnp.where(left, early, swapped_late).astype(bf16)
    rim_copy = pltpu.make_async_remote_copy(
        src_ref=rim_sent,
        dst_ref=rim_got,
        send_sem=rim_sem.at[0],
        recv_sem=rim_sem.at[1],
        device_id=(blk, me - 1),
        device_id_type=MESH,
    )

    @pl.when(me > 0)
    def _():
        rim_copy.start()

    middle, end = EDGE + half_len, EDGE + block_len
    ext[0, EDGE:middle] = early
    ext[0, middle:end] = late
    ext[1, EDGE:middle] = swapped_early
    ext[1, middle:end] = swapped_late

    tops = (end, 0)

    def take_edge(side, beside):
        here = leaves[1 - side]

        @pl.when(here & (me < devices - 1) if beside else here)
        def _():
            edges[side, beside].wait_recv()

        @pl.when(jnp.logical_not(here & (me < devices - 1) if beside else here))
        def _():
            edge_got[beside, side] = jnp.zeros(edge_got.shape[2:], bf16)

    span = shifted.shape[2]
    tiles = span // (2 * PHASE)

    def shift_rows(a):
        for r in range(PHASE):
            begin = EDGE - RIM + 1 + r
            halves = [
                ext[a, begin + place : begin + place + span].reshape(tiles, 2, PHASE, local_ch)
                for place in (0, half_len)
            ]
            for odd in range(2):
                pair = jnp.stack([halves[0][:, odd], halves[1][:, odd]], axis=1)
                shifted[a, odd, :, r * local_ch : (r + 1) * local_ch] = pair.reshape(span, local_ch).astype(bf16)

    depth = PHASE * SUBARRAY

    def beam(a):
        for first in range(0, half_len, TURNS):
            total = None
            for g in range(weights.shape[0] // depth):
                top = first + 2 * PHASE * (g // 2)
                part = dot_f32(shifted[a, g % 2, top : top + TURNS], weights[g * depth : (g + 1) * depth])
                total = part if total is None else total + part
            count = TURNS // (2 * PHASE)
            parts = total.reshape(count, 2, PHASE, 2 * slow_count)
            for half in range(2):
                pair = jnp.stack([parts[:, half, :, :slow_count], parts[:, half, :, slow_count:]], axis=1)
                lanes = half * half_len + first
                out_ref[a, :, lanes : lanes + TURNS] = pair.reshape(TURNS, slow_count).T.astype(bf16)

    for side in range(2):
        take_edge(side, 0)
        ext[0, tops[side] : tops[side] + EDGE] = edge_got[0, side].astype(f32)
    shift_rows(0)
    beam(0)

    for side in range(2):
        take_edge(side, 1)
        own = pltpu.roll(edge_got[0, side].astype(f32), STRIDE, 1)
        other = pltpu.roll(edge_got[1, side].astype(f32), STRIDE, 1)
        ext[1, tops[side] : tops[side] + EDGE] = jnp.where(left[:EDGE], own, other)

    @pl.when(me < devices - 1)
    def _():
        rim_copy.wait_recv()

    @pl.when(is_last)
    def _():
        rim_got[...] = jnp.zeros(rim_got.shape, bf16)

    rim = rim_got[...].astype(f32)
    ext[1, EDGE:middle] = jnp.where(left, ext[1, EDGE:middle], pltpu.roll(rim, STRIDE, 1))
    ext[1, middle:end] = jnp.where(left, ext[1, middle:end], rim)
    shift_rows(1)
    beam(1)

    drain_exchanges()
    for side in range(2):
        for beside in range(2):

            @pl.when(leaves[side] & (me > 0) if beside else leaves[side])
            def _():
                edges[side, beside].wait_send()

    @pl.when(me > 0)
    def _():
        rim_copy.wait_send()


def fused_body(devices, blocks, record, fk_mask, tap_table, delay_whole, tap_index):
    block_len, local_ch = record.shape
    band_rows, channels = fk_mask.shape
    slow_count = delay_whole.shape[0]
    half_len, half_rows = block_len // 2, band_rows // 2
    ahead, behind = parity_tables(block_len, devices)
    cos_twist, sin_twist = twist_tables(devices, local_ch)
    mix = local_table(local_ch)
    subarrays = local_ch // STRIDE
    span = half_len + EDGE
    bf16 = jnp.bfloat16
    vmem = pl.BlockSpec(memory_space=pltpu.VMEM)
    hbm = pl.BlockSpec(memory_space=pltpu.HBM)
    return pl.pallas_call(
        functools.partial(fused, devices, blocks),
        out_shape=pltpu.VMEM((subarrays, slow_count, block_len), bf16),
        in_specs=[vmem] + [hbm] * 10,
        out_specs=vmem,
        scratch_shapes=[
            pltpu.VMEM((block_len, local_ch), jnp.float32),
            pltpu.VMEM((band_rows, channels), jnp.int32),
            pltpu.VMEM((slow_count, SUBARRAY), jnp.int32),
            pltpu.VMEM((slow_count, SUBARRAY), jnp.int32),
            pltpu.VMEM((6 * local_ch, 2 * local_ch), bf16),
            pltpu.VMEM((6 * local_ch, 2 * local_ch), bf16),
            pltpu.VMEM((devices, local_ch), jnp.float32),
            pltpu.VMEM((devices, local_ch), jnp.float32),
            pltpu.VMEM(ahead.shape, bf16),
            pltpu.VMEM(behind.shape, bf16),
            pltpu.VMEM((block_len, 2 * local_ch), bf16),
            pltpu.VMEM((2, devices, band_rows, local_ch), bf16),
            pltpu.VMEM((2, devices, band_rows, local_ch), bf16),
            pltpu.VMEM((devices * half_rows, 2 * local_ch), jnp.float32),
            pltpu.VMEM((2, devices * half_rows, local_ch), jnp.float32),
            pltpu.VMEM((2, devices, band_rows, local_ch), bf16),
            pltpu.VMEM((2, devices, band_rows, local_ch), bf16),
            pltpu.VMEM((subarrays, block_len + 2 * EDGE, local_ch), jnp.float32),
            pltpu.VMEM((2, EDGE, local_ch), bf16),
            pltpu.VMEM((2, 2, EDGE, local_ch), bf16),
            pltpu.VMEM((half_len, local_ch), bf16),
            pltpu.VMEM((half_len, local_ch), bf16),
            pltpu.VMEM(((LAGS + PHASE) * SUBARRAY, 2 * slow_count), bf16),
            pltpu.VMEM((subarrays, 2, span, PHASE * local_ch), bf16),
            pltpu.SemaphoreType.DMA((8,)),
            pltpu.SemaphoreType.DMA((3,)),
            pltpu.SemaphoreType.DMA((2, 2, devices)),
            pltpu.SemaphoreType.DMA((2, 2, devices)),
            pltpu.SemaphoreType.DMA((2, 2)),
            pltpu.SemaphoreType.DMA((2, 2)),
            pltpu.SemaphoreType.DMA((2,)),
        ],
        compiler_params=pltpu.CompilerParams(
            collective_id=0, has_side_effects=True, vmem_limit_bytes=60 * 2**20
        ),
    )(
        tap_table,
        record,
        fk_mask,
        delay_whole,
        tap_index,
        jnp.asarray(triple(mix)),
        jnp.asarray(triple(mix.T)),
        jnp.asarray(cos_twist),
        jnp.asarray(sin_twist),
        jnp.asarray(ahead),
        jnp.asarray(behind),
    )


def solution(mesh):
    placed = (P("tm", "chan"), P("chan", None), P(), P(), P())
    devices, blocks = mesh.shape["chan"], mesh.shape["tm"]

    def placed_body(record, *others):
        block_len, local_ch = record.shape
        if local_ch == TILE and block_len // devices == TILE:
            return fused_body(devices, blocks, record, *others)
        return body(record, *others)

    return jax.shard_map(
        placed_body, mesh=mesh, in_specs=placed, out_specs=P("chan", None, "tm"), check_vma=False
    )
```

time: 31.2 us -> 24 us (0.77)
  Pallas kernels: 30.2 us -> 23 us
    pallas_call x1, Pallas kernels: 30.2 us -> 23 us  [fused_body(): pl.pallas_call(functools.partial(fused, devices, blocks), out_shape=pltpu...]
where the time goes in v2:
time: 24 us; the launch traced here: 23.8 us
  Pallas kernels  23 us (96%)
  local copies, waits for them, and re-layouts  0.8 us (3%)
    pallas_call x1, Pallas kernels, fused_body(): pl.pallas_call(functools.partial(fused, devices, blocks), out_shape=pltpu...  23 us
    unnamed x1, local copies, waits for them, and re-layouts  0.8 us

profile of v2, /device:TPU:0, one launch (start us, length us, event | category | flops | bytes accessed | tf_op | source)
XLA Modules:
  0.0 23.8 jit_solution(12473552697265144277)
XLA Ops:
  0.0 23.0 %shard_map.109 = bf16[2,128,1024]{2,1,0:T(8,128)(2,1)S(1)} custom-call(bf16[8,8]{1,0:T(8,128)(2,1)} %tap_ref.1, f32[1024,128]{1,0:T(8,128)} %rec_hbm.1, s32[64,1024]{1,0:T(8,128)} %mask_hbm.1, s32[128,128]{1,0:T(8,128)} %delay_hbm.1, s32[128,128]{1,0:T(8,128)} %index_hbm.1, bf16[768,256]{1,0:T(8,128)(2,1)} %constant.12.clone.mix_hbm, ...), custom_call_target="tpu_custom_call" | custom-call | tf_op jit(solution)/shard_map/pallas_call | solution.py:623
  23.0 0.8 %copy.13 = bf16[2,128,1024]{2,1,0:T(8,128)(2,1)} copy(bf16[2,128,1024]{2,1,0:T(8,128)(2,1)S(1)} %shard_map.109) | data formatting | bytes 1048576

commit v3 on v2

--- a/solution.py
+++ b/solution.py
@@ -185,8 +185,8 @@
 
 TILE = 128
 EDGE = 32
+LEAD = 8
 PHASE = 8
-TURNS = 2 * TILE
 MESH = pl.DeviceIdType.MESH
 
 
@@ -227,7 +227,7 @@
 def fused(
     devices,
     blocks,
-    tap_ref,
+    tap_hbm,
     rec_hbm,
     mask_hbm,
     delay_hbm,
@@ -239,6 +239,7 @@
     ahead_hbm,
     behind_hbm,
     out_ref,
+    tap_ref,
     rec_ref,
     mask_ref,
     delay_ref,
@@ -263,6 +264,8 @@
     rim_got,
     weights,
     shifted,
+    partial,
+    sums,
     load_sem,
     table_sem,
     send_sem,
@@ -292,6 +295,7 @@
         for place, (source, target) in enumerate(
             (
                 (rec_hbm, rec_ref),
+                (tap_hbm, tap_ref),
                 (mask_hbm, mask_ref),
                 (delay_hbm, delay_ref),
                 (index_hbm, index_ref),
@@ -452,9 +456,10 @@
     table = tap_ref[...].astype(f32)
     starts = delay_ref[...].astype(f32).T.astype(jnp.int32) + LAG
     index_t = index_ref[...].astype(f32).T.astype(jnp.int32)
-    blank = jnp.zeros((PHASE * SUBARRAY, slow_count), bf16)
-    weights[LAGS * SUBARRAY :, :slow_count] = blank
-    weights[: PHASE * SUBARRAY, slow_count:] = blank
+    blank = jnp.zeros((PHASE * STRIDE, slow_count), bf16)
+    for part in range(2):
+        weights[part, LAGS * STRIDE :, :slow_count] = blank
+        weights[part, : PHASE * STRIDE, slow_count:] = blank
     for first in range(0, SUBARRAY, 32):
         start = starts[first : first + 32]
         index = index_t[first : first + 32]
@@ -471,8 +476,9 @@
                     value = jnp.where(start == lag - tap_pos, coeffs[tap_pos], value)
             value = value.astype(bf16)
             for phase in range(2):
-                top = (lag + PHASE * phase) * SUBARRAY + first
-                weights[top : top + 32, phase * slow_count : (phase + 1) * slow_count] = value
+                part, place = divmod(first, STRIDE)
+                top = (lag + PHASE * phase) * STRIDE + place
+                weights[part, top : top + 32, phase * slow_count : (phase + 1) * slow_count] = value
     pieces = []
     for parity in range(2):
         for k in order:
@@ -519,13 +525,13 @@
     def _():
         rim_copy.start()
 
-    middle, end = EDGE + half_len, EDGE + block_len
-    ext[0, EDGE:middle] = early
-    ext[0, middle:end] = late
-    ext[1, EDGE:middle] = swapped_early
-    ext[1, middle:end] = swapped_late
-
-    tops = (end, 0)
+    top, middle, end = LEAD + EDGE, LEAD + EDGE + half_len, LEAD + EDGE + block_len
+    for group, (plain, other) in enumerate((((early, late), (swapped_early, swapped_late)),) * 2):
+        low_part, next_part = (other, plain) if group else (plain, other)
+        for place, rows in enumerate(((top, middle), (middle, end))):
+            ext[group, rows[0] - 1 : rows[1] - 1] = next_part[place]
+        for place, rows in enumerate(((top, middle), (middle, end))):
+            ext[group, rows[0] : rows[1], :STRIDE] = low_part[place][:, :STRIDE]
 
     def take_edge(side, beside):
         here = leaves[1 - side]
@@ -538,47 +544,77 @@
         def _():
             edge_got[beside, side] = jnp.zeros(edge_got.shape[2:], bf16)
 
-    span = shifted.shape[2]
-    tiles = span // (2 * PHASE)
-
-    def shift_rows(a):
-        for r in range(PHASE):
-            begin = EDGE - RIM + 1 + r
-            halves = [
-                ext[a, begin + place : begin + place + span].reshape(tiles, 2, PHASE, local_ch)
-                for place in (0, half_len)
+    def put_edge(side, beside):
+        begin = (end, LEAD)[side]
+        plain = edge_got[beside, side].astype(f32)
+        other = pltpu.roll(plain, STRIDE, 1)
+        for group in ((2,) if beside else (0, 1)):
+            low_part, next_part = (other, plain) if group == 1 else (plain, other)
+            before = slice(begin - 1, begin - 1 + EDGE)
+            ext[group, before] = jnp.where(left[:EDGE], ext[group, before], next_part)
+            ext[group, begin : begin + EDGE, :STRIDE] = low_part[:, :STRIDE]
+
+    pairs = PHASE // 2
+
+    def shift_rows(group, row, count):
+        for i in range(pairs):
+            halves = []
+            for place in (0, half_len):
+                begin = top - RIM + 1 + 2 * i + row + place
+                value = ext[group, begin : begin + count]
+                halves.append(value.reshape(count // (2 * PHASE), 2, PHASE, local_ch))
+            for odd in range(2):
+                pair = jnp.stack([halves[0][:, odd], halves[1][:, odd]], axis=1).reshape(count, local_ch)
+                shifted[group, odd, row : row + count, i * local_ch : (i + 1) * local_ch] = pair.astype(bf16)
+
+    steps = weights.shape[1] // (PHASE * STRIDE)
+    core = half_len - 2 * EDGE
+    inside = ((EDGE, core),)
+    outside = ((0, EDGE), (half_len - EDGE, EDGE))
+
+    def operand(chosen):
+        columns = []
+        for g in range(steps):
+            low_row = 2 * PHASE * (g // 2)
+            pieces = [
+                shifted[group, g % 2, first + low_row : first + low_row + count]
+                for group, spans in chosen
+                for first, count in spans
             ]
-            for odd in range(2):
-                pair = jnp.stack([halves[0][:, odd], halves[1][:, odd]], axis=1)
-                shifted[a, odd, :, r * local_ch : (r + 1) * local_ch] = pair.reshape(span, local_ch).astype(bf16)
-
-    depth = PHASE * SUBARRAY
-
-    def beam(a):
-        for first in range(0, half_len, TURNS):
-            total = None
-            for g in range(weights.shape[0] // depth):
-                top = first + 2 * PHASE * (g // 2)
-                part = dot_f32(shifted[a, g % 2, top : top + TURNS], weights[g * depth : (g + 1) * depth])
-                total = part if total is None else total + part
-            count = TURNS // (2 * PHASE)
-            parts = total.reshape(count, 2, PHASE, 2 * slow_count)
+            columns.append(pieces[0] if len(pieces) == 1 else jnp.concatenate(pieces, axis=0))
+        return jnp.concatenate(columns, axis=1)
+
+    def keep_sums(a, total, spans):
+        taken = 0
+        for first, count in spans:
+            parts = total[taken : taken + count].reshape(count // (2 * PHASE), 2, PHASE, 2 * slow_count)
             for half in range(2):
                 pair = jnp.stack([parts[:, half, :, :slow_count], parts[:, half, :, slow_count:]], axis=1)
-                lanes = half * half_len + first
-                out_ref[a, :, lanes : lanes + TURNS] = pair.reshape(TURNS, slow_count).T.astype(bf16)
-
-    for side in range(2):
-        take_edge(side, 0)
-        ext[0, tops[side] : tops[side] + EDGE] = edge_got[0, side].astype(f32)
-    shift_rows(0)
-    beam(0)
-
-    for side in range(2):
-        take_edge(side, 1)
-        own = pltpu.roll(edge_got[0, side].astype(f32), STRIDE, 1)
-        other = pltpu.roll(edge_got[1, side].astype(f32), STRIDE, 1)
-        ext[1, tops[side] : tops[side] + EDGE] = jnp.where(left[:EDGE], own, other)
+                sums[a, half, first : first + count] = pair.reshape(count, slow_count)
+            taken += count
+
+    def put(a, first, count):
+        for half in range(2):
+            lanes = half * half_len + first
+            out_ref[a, :, lanes : lanes + count] = sums[a, half, first : first + count].T.astype(bf16)
+
+    first_rows, half_core = EDGE, core // 2
+    shift_rows(0, EDGE, half_core + EDGE)
+    shift_rows(1, EDGE, half_core + EDGE)
+    chunk = ((EDGE, half_core),)
+    total = dot_f32(operand([(0, chunk)]), weights[0]) + dot_f32(operand([(1, chunk)]), weights[1])
+    shift_rows(0, half_core + 2 * EDGE, half_core)
+    keep_sums(0, total, chunk)
+    shift_rows(1, half_core + 2 * EDGE, half_core)
+    chunk = ((EDGE + half_core, half_core),)
+    total = dot_f32(operand([(0, chunk)]), weights[0]) + dot_f32(operand([(1, chunk)]), weights[1])
+    keep_sums(0, total, chunk)
+    partial[...] = dot_f32(operand([(1, inside)]), weights[0])
+    put(0, TILE, half_len - 2 * TILE)
+
+    for beside in range(2):
+        for side in range(2):
+            take_edge(side, beside)
 
     @pl.when(me < devices - 1)
     def _():
@@ -588,11 +624,33 @@
     def _():
         rim_got[...] = jnp.zeros(rim_got.shape, bf16)
 
+    for side in range(2):
+        put_edge(side, 0)
+    for group in range(2):
+        for row in (0, half_len):
+            shift_rows(group, row, EDGE)
+    around = dot_f32(operand([(0, outside), (1, outside)]), weights[0])
     rim = rim_got[...].astype(f32)
-    ext[1, EDGE:middle] = jnp.where(left, ext[1, EDGE:middle], pltpu.roll(rim, STRIDE, 1))
-    ext[1, middle:end] = jnp.where(left, ext[1, middle:end], rim)
-    shift_rows(1)
-    beam(1)
+    swapped_rim = pltpu.roll(rim, STRIDE, 1)
+    ext[2, top - 1 : middle - 1] = swapped_rim
+    ext[2, middle - 1 : end - 1] = rim
+    ext[2, top:middle, :STRIDE] = rim[:, :STRIDE]
+    ext[2, middle:end, :STRIDE] = swapped_rim[:, :STRIDE]
+    for side in range(2):
+        put_edge(side, 1)
+    shift_rows(2, 0, half_len + EDGE)
+    cut = 2 * EDGE
+    firsts, lasts = ((EDGE, core // 2),), ((EDGE + core // 2, core // 2),)
+    more = dot_f32(operand([(1, outside), (2, outside), (2, firsts)]), weights[1])
+    keep_sums(0, around[:cut] + more[:cut], outside)
+    keep_sums(1, around[cut:] + more[cut : 2 * cut], outside)
+    keep_sums(1, partial[: core // 2] + more[2 * cut :], firsts)
+    more = dot_f32(operand([(2, lasts)]), weights[1])
+    for first in (0, half_len - TILE):
+        put(0, first, TILE)
+    put(1, 0, 2 * TILE)
+    keep_sums(1, partial[core // 2 :] + more, lasts)
+    put(1, 2 * TILE, half_len - 2 * TILE)
 
     drain_exchanges()
     for side in range(2):
@@ -623,9 +681,10 @@
     return pl.pallas_call(
         functools.partial(fused, devices, blocks),
         out_shape=pltpu.VMEM((subarrays, slow_count, block_len), bf16),
-        in_specs=[vmem] + [hbm] * 10,
+        in_specs=[hbm] * 11,
         out_specs=vmem,
         scratch_shapes=[
+            pltpu.VMEM(tap_table.shape, bf16),
             pltpu.VMEM((block_len, local_ch), jnp.float32),
             pltpu.VMEM((band_rows, channels), jnp.int32),
             pltpu.VMEM((slow_count, SUBARRAY), jnp.int32),
@@ -643,14 +702,16 @@
             pltpu.VMEM((2, devices * half_rows, local_ch), jnp.float32),
             pltpu.VMEM((2, devices, band_rows, local_ch), bf16),
             pltpu.VMEM((2, devices, band_rows, local_ch), bf16),
-            pltpu.VMEM((subarrays, block_len + 2 * EDGE, local_ch), jnp.float32),
+            pltpu.VMEM((3, LEAD + block_len + 2 * EDGE, local_ch), jnp.float32),
             pltpu.VMEM((2, EDGE, local_ch), bf16),
             pltpu.VMEM((2, 2, EDGE, local_ch), bf16),
             pltpu.VMEM((half_len, local_ch), bf16),
             pltpu.VMEM((half_len, local_ch), bf16),
-            pltpu.VMEM(((LAGS + PHASE) * SUBARRAY, 2 * slow_count), bf16),
-            pltpu.VMEM((subarrays, 2, span, PHASE * local_ch), bf16),
-            pltpu.SemaphoreType.DMA((8,)),
+            pltpu.VMEM((2, (LAGS + PHASE) * STRIDE, 2 * slow_count), bf16),
+            pltpu.VMEM((3, 2, span, PHASE * STRIDE), bf16),
+            pltpu.VMEM((half_len - 2 * EDGE, 2 * slow_count), jnp.float32),
+            pltpu.VMEM((subarrays, 2, half_len, slow_count), jnp.float32),
+            pltpu.SemaphoreType.DMA((9,)),
             pltpu.SemaphoreType.DMA((3,)),
             pltpu.SemaphoreType.DMA((2, 2, devices)),
             pltpu.SemaphoreType.DMA((2, 2, devices)),

time: 24 us -> 21.7 us (0.904)
  the two profiles are of different devices: /device:TPU:0 before, /device:TPU:1 now
where the time goes in v3:
time: 21.7 us; the launch traced here: 21.6 us
  Pallas kernels  20.8 us (96%)
  local copies, waits for them, and re-layouts  0.8 us (4%)
    pallas_call x1, Pallas kernels, fused_body(): pl.pallas_call(functools.partial(fused, devices, blocks), out_shape=pltpu...  20.8 us
    unnamed x1, local copies, waits for them, and re-layouts  0.8 us

profile of v3, /device:TPU:1, one launch (start us, length us, event | category | flops | bytes accessed | tf_op | source)
XLA Modules:
  0.0 21.6 jit_solution(17123484737942436002)
XLA Ops:
  0.0 20.8 %shard_map.109 = bf16[2,128,1024]{2,1,0:T(8,128)(2,1)S(1)} custom-call(bf16[8,8]{1,0:T(8,128)(2,1)} %tap_hbm.1, f32[1024,128]{1,0:T(8,128)} %rec_hbm.1, s32[64,1024]{1,0:T(8,128)} %mask_hbm.1, s32[128,128]{1,0:T(8,128)} %delay_hbm.1, s32[128,128]{1,0:T(8,128)} %index_hbm.1, bf16[768,256]{1,0:T(8,128)(2,1)} %constant.12.clone.mix_hbm, ...), custom_call_target="tpu_custom_call" | custom-call | tf_op jit(solution)/shard_map/pallas_call | solution.py:681
  20.8 0.8 %copy.13 = bf16[2,128,1024]{2,1,0:T(8,128)(2,1)} copy(bf16[2,128,1024]{2,1,0:T(8,128)(2,1)S(1)} %shard_map.109) | data formatting | bytes 1048576

commit v4 on v3

--- a/solution.py
+++ b/solution.py
@@ -479,15 +479,16 @@
                 part, place = divmod(first, STRIDE)
                 top = (lag + PHASE * phase) * STRIDE + place
                 weights[part, top : top + 32, phase * slow_count : (phase + 1) * slow_count] = value
-    pieces = []
     for parity in range(2):
         for k in order:
             back_copies[parity, k].wait_recv()
         rows = back_got[parity].reshape(half_len, local_ch)
-        pieces.append(dot_f32(behind[parity], jnp.concatenate([rows, rows], axis=0)))
-    early, late = pieces[0] + pieces[1], pieces[0] - pieces[1]
-    edge_sent[0] = early[:EDGE].astype(bf16)
-    edge_sent[1] = late[half_len - EDGE :].astype(bf16)
+        if parity == 0:
+            even = dot_f32(behind[0], jnp.concatenate([rows, rows], axis=0))
+    at_edge = jnp.concatenate([behind[1, :EDGE, :half_len], behind[1, half_len - EDGE :, :half_len]], axis=0)
+    odd_edge = dot_f32(at_edge, rows)
+    edge_sent[0] = (even[:EDGE] + odd_edge[:EDGE]).astype(bf16)
+    edge_sent[1] = (even[half_len - EDGE :] - odd_edge[EDGE:]).astype(bf16)
 
     def edge_copy(side, beside):
         return pltpu.make_async_remote_copy(
@@ -508,23 +509,31 @@
             def _():
                 edges[side, beside].start()
 
-    swapped_early = pltpu.roll(early, STRIDE, 1)
-    swapped_late = pltpu.roll(late, STRIDE, 1)
-    left = lax.broadcasted_iota(jnp.int32, (half_len, local_ch), 1) < STRIDE
-    rim_sent[...] = jnp.where(left, early, swapped_late).astype(bf16)
-    rim_copy = pltpu.make_async_remote_copy(
-        src_ref=rim_sent,
-        dst_ref=rim_got,
-        send_sem=rim_sem.at[0],
-        recv_sem=rim_sem.at[1],
-        device_id=(blk, me - 1),
-        device_id_type=MESH,
-    )
-
-    @pl.when(me > 0)
-    def _():
-        rim_copy.start()
-
+    quarter = half_len // 2
+    left = lax.broadcasted_iota(jnp.int32, (quarter, local_ch), 1) < STRIDE
+    rim_copies, fields = [], []
+    for first in (0, quarter):
+        odd = dot_f32(behind[1, first : first + quarter, :half_len], rows)
+        some = even[first : first + quarter]
+        field = [some + odd, some - odd]
+        field += [pltpu.roll(part, STRIDE, 1) for part in field]
+        fields.append(field)
+        rim_sent[first : first + quarter] = jnp.where(left, field[0], field[3]).astype(bf16)
+        copy = pltpu.make_async_remote_copy(
+            src_ref=rim_sent.at[first : first + quarter],
+            dst_ref=rim_got.at[first : first + quarter],
+            send_sem=rim_sem.at[0, len(rim_copies)],
+            recv_sem=rim_sem.at[1, len(rim_copies)],
+            device_id=(blk, me - 1),
+            device_id_type=MESH,
+        )
+        rim_copies.append(copy)
+
+        @pl.when(me > 0)
+        def _():
+            copy.start()
+
+    early, late, swapped_early, swapped_late = [jnp.concatenate(parts, axis=0) for parts in zip(*fields)]
     top, middle, end = LEAD + EDGE, LEAD + EDGE + half_len, LEAD + EDGE + block_len
     for group, (plain, other) in enumerate((((early, late), (swapped_early, swapped_late)),) * 2):
         low_part, next_part = (other, plain) if group else (plain, other)
@@ -598,7 +607,7 @@
             lanes = half * half_len + first
             out_ref[a, :, lanes : lanes + count] = sums[a, half, first : first + count].T.astype(bf16)
 
-    first_rows, half_core = EDGE, core // 2
+    half_core = core // 2
     shift_rows(0, EDGE, half_core + EDGE)
     shift_rows(1, EDGE, half_core + EDGE)
     chunk = ((EDGE, half_core),)
@@ -618,7 +627,8 @@
 
     @pl.when(me < devices - 1)
     def _():
-        rim_copy.wait_recv()
+        for copy in rim_copies:
+            copy.wait_recv()
 
     @pl.when(is_last)
     def _():
@@ -640,17 +650,18 @@
         put_edge(side, 1)
     shift_rows(2, 0, half_len + EDGE)
     cut = 2 * EDGE
-    firsts, lasts = ((EDGE, core // 2),), ((EDGE + core // 2, core // 2),)
+    many = half_len - TILE - EDGE
+    firsts, lasts = ((EDGE, many),), ((EDGE + many, core - many),)
     more = dot_f32(operand([(1, outside), (2, outside), (2, firsts)]), weights[1])
     keep_sums(0, around[:cut] + more[:cut], outside)
     keep_sums(1, around[cut:] + more[cut : 2 * cut], outside)
-    keep_sums(1, partial[: core // 2] + more[2 * cut :], firsts)
+    keep_sums(1, partial[:many] + more[2 * cut :], firsts)
     more = dot_f32(operand([(2, lasts)]), weights[1])
     for first in (0, half_len - TILE):
         put(0, first, TILE)
-    put(1, 0, 2 * TILE)
-    keep_sums(1, partial[core // 2 :] + more, lasts)
-    put(1, 2 * TILE, half_len - 2 * TILE)
+    put(1, 0, half_len - TILE)
+    keep_sums(1, partial[many:] + more, lasts)
+    put(1, half_len - TILE, TILE)
 
     drain_exchanges()
     for side in range(2):
@@ -662,7 +673,8 @@
 
     @pl.when(me > 0)
     def _():
-        rim_copy.wait_send()
+        for copy in rim_copies:
+            copy.wait_send()
 
 
 def fused_body(devices, blocks, record, fk_mask, tap_table, delay_whole, tap_index):
@@ -717,7 +729,7 @@
             pltpu.SemaphoreType.DMA((2, 2, devices)),
             pltpu.SemaphoreType.DMA((2, 2)),
             pltpu.SemaphoreType.DMA((2, 2)),
-            pltpu.SemaphoreType.DMA((2,)),
+            pltpu.SemaphoreType.DMA((2, 2)),
         ],
         compiler_params=pltpu.CompilerParams(
             collective_id=0, has_side_effects=True, vmem_limit_bytes=60 * 2**20

time: 21.7 us -> 20.9 us (0.963)
  the two profiles are of different devices: /device:TPU:1 before, /device:TPU:0 now
where the time goes in v4:
time: 20.9 us; the launch traced here: 20.8 us
  Pallas kernels  20 us (96%)
  local copies, waits for them, and re-layouts  0.8 us (4%)
    pallas_call x1, Pallas kernels, fused_body(): pl.pallas_call(functools.partial(fused, devices, blocks), out_shape=pltpu...  20 us
    unnamed x1, local copies, waits for them, and re-layouts  0.8 us

profile of v4, /device:TPU:0, one launch (start us, length us, event | category | flops | bytes accessed | tf_op | source)
XLA Modules:
  0.0 20.8 jit_solution(5009259016284606812)
XLA Ops:
  0.0 20.0 %shard_map.109 = bf16[2,128,1024]{2,1,0:T(8,128)(2,1)S(1)} custom-call(bf16[8,8]{1,0:T(8,128)(2,1)} %tap_hbm.1, f32[1024,128]{1,0:T(8,128)} %rec_hbm.1, s32[64,1024]{1,0:T(8,128)} %mask_hbm.1, s32[128,128]{1,0:T(8,128)} %delay_hbm.1, s32[128,128]{1,0:T(8,128)} %index_hbm.1, bf16[768,256]{1,0:T(8,128)(2,1)} %constant.12.clone.mix_hbm, ...), custom_call_target="tpu_custom_call" | custom-call | tf_op jit(solution)/shard_map/pallas_call | solution.py:693
  20.0 0.8 %copy.13 = bf16[2,128,1024]{2,1,0:T(8,128)(2,1)} copy(bf16[2,128,1024]{2,1,0:T(8,128)(2,1)S(1)} %shard_map.109) | data formatting | bytes 1048576

commit v5 on v4

--- a/solution.py
+++ b/solution.py
@@ -485,11 +485,6 @@
         rows = back_got[parity].reshape(half_len, local_ch)
         if parity == 0:
             even = dot_f32(behind[0], jnp.concatenate([rows, rows], axis=0))
-    at_edge = jnp.concatenate([behind[1, :EDGE, :half_len], behind[1, half_len - EDGE :, :half_len]], axis=0)
-    odd_edge = dot_f32(at_edge, rows)
-    edge_sent[0] = (even[:EDGE] + odd_edge[:EDGE]).astype(bf16)
-    edge_sent[1] = (even[half_len - EDGE :] - odd_edge[EDGE:]).astype(bf16)
-
     def edge_copy(side, beside):
         return pltpu.make_async_remote_copy(
             src_ref=edge_sent.at[side],
@@ -502,13 +497,6 @@
 
     edges = {(side, beside): edge_copy(side, beside) for side in range(2) for beside in range(2)}
     leaves = (low_blk, high_blk)
-    for side in range(2):
-        for beside in range(2):
-
-            @pl.when(leaves[side] & (me > 0) if beside else leaves[side])
-            def _():
-                edges[side, beside].start()
-
     quarter = half_len // 2
     left = lax.broadcasted_iota(jnp.int32, (quarter, local_ch), 1) < STRIDE
     rim_copies, fields = [], []
@@ -534,6 +522,15 @@
             copy.start()
 
     early, late, swapped_early, swapped_late = [jnp.concatenate(parts, axis=0) for parts in zip(*fields)]
+    edge_sent[0] = early[:EDGE].astype(bf16)
+    edge_sent[1] = late[half_len - EDGE :].astype(bf16)
+    for side in range(2):
+        for beside in range(2):
+
+            @pl.when(leaves[side] & (me > 0) if beside else leaves[side])
+            def _():
+                edges[side, beside].start()
+
     top, middle, end = LEAD + EDGE, LEAD + EDGE + half_len, LEAD + EDGE + block_len
     for group, (plain, other) in enumerate((((early, late), (swapped_early, swapped_late)),) * 2):
         low_part, next_part = (other, plain) if group else (plain, other)
@@ -648,11 +645,13 @@
     ext[2, middle:end, :STRIDE] = swapped_rim[:, :STRIDE]
     for side in range(2):
         put_edge(side, 1)
-    shift_rows(2, 0, half_len + EDGE)
+    shift_rows(2, 0, half_len - TILE + 2 * EDGE)
+    shift_rows(2, half_len - EDGE, 2 * EDGE)
     cut = 2 * EDGE
     many = half_len - TILE - EDGE
     firsts, lasts = ((EDGE, many),), ((EDGE + many, core - many),)
     more = dot_f32(operand([(1, outside), (2, outside), (2, firsts)]), weights[1])
+    shift_rows(2, half_len - TILE + 2 * EDGE, TILE - 3 * EDGE)
     keep_sums(0, around[:cut] + more[:cut], outside)
     keep_sums(1, around[cut:] + more[cut : 2 * cut], outside)
     keep_sums(1, partial[:many] + more[2 * cut :], firsts)

time: 20.9 us -> 20.7 us (level)
  no operation moved by 1% of the time
where the time goes in v5:
time: 20.7 us; the launch traced here: 20.6 us
  Pallas kernels  19.8 us (96%)
  local copies, waits for them, and re-layouts  0.8 us (4%)
    pallas_call x1, Pallas kernels, fused_body(): pl.pallas_call(functools.partial(fused, devices, blocks), out_shape=pltpu...  19.8 us
    unnamed x1, local copies, waits for them, and re-layouts  0.8 us

profile of v5, /device:TPU:0, one launch (start us, length us, event | category | flops | bytes accessed | tf_op | source)
XLA Modules:
  0.0 20.6 jit_solution(17912069341380318972)
XLA Ops:
  0.0 19.8 %shard_map.109 = bf16[2,128,1024]{2,1,0:T(8,128)(2,1)S(1)} custom-call(bf16[8,8]{1,0:T(8,128)(2,1)} %tap_hbm.1, f32[1024,128]{1,0:T(8,128)} %rec_hbm.1, s32[64,1024]{1,0:T(8,128)} %mask_hbm.1, s32[128,128]{1,0:T(8,128)} %delay_hbm.1, s32[128,128]{1,0:T(8,128)} %index_hbm.1, bf16[768,256]{1,0:T(8,128)(2,1)} %constant.12.clone.mix_hbm, ...), custom_call_target="tpu_custom_call" | custom-call | tf_op jit(solution)/shard_map/pallas_call | solution.py:692
  19.8 0.8 %copy.13 = bf16[2,128,1024]{2,1,0:T(8,128)(2,1)} copy(bf16[2,128,1024]{2,1,0:T(8,128)(2,1)S(1)} %shard_map.109) | data formatting | bytes 1048576

commit v6 on v4

--- a/solution.py
+++ b/solution.py
@@ -342,16 +342,15 @@
         high = value.astype(bf16)
         folded[:half_len, :local_ch] = high
         folded[:half_len, local_ch:] = (value - high.astype(f32)).astype(bf16)
-        folded[half_len:, :local_ch] = high
-        folded[half_len:, local_ch:] = jnp.zeros_like(high)
 
     copies = {}
     loads[0].wait()
     for parity in range(2):
         fold(parity)
         tables[parity].wait()
-        both = dot_f32(ahead[parity], folded[...])
-        part = (both[:, :local_ch] + both[:, local_ch:]).astype(bf16)
+        both = dot_f32(ahead[parity, :, :half_len], folded[...])
+        low = dot_f32(ahead[parity, :, half_len:], folded[:, :local_ch])
+        part = (both[:, :local_ch] + both[:, local_ch:] + low).astype(bf16)
         sent[parity] = part.reshape(devices, band_rows, local_ch)
         if parity == 0:
             neighbours = count_of(low_blk) + count_of(high_blk)
@@ -707,7 +706,7 @@
             pltpu.VMEM((devices, local_ch), jnp.float32),
             pltpu.VMEM(ahead.shape, bf16),
             pltpu.VMEM(behind.shape, bf16),
-            pltpu.VMEM((block_len, 2 * local_ch), bf16),
+            pltpu.VMEM((half_len, 2 * local_ch), bf16),
             pltpu.VMEM((2, devices, band_rows, local_ch), bf16),
             pltpu.VMEM((2, devices, band_rows, local_ch), bf16),
             pltpu.VMEM((devices * half_rows, 2 * local_ch), jnp.float32),

time: 20.9 us -> 20.9 us (level)
  no operation moved by 1% of the time
where the time goes in v6:
time: 20.9 us; the launch traced here: 20.8 us
  Pallas kernels  19.9 us (95%)
  local copies, waits for them, and re-layouts  0.8 us (4%)
    pallas_call x1, Pallas kernels, fused_body(): pl.pallas_call(functools.partial(fused, devices, blocks), out_shape=pltpu...  19.9 us
    unnamed x1, local copies, waits for them, and re-layouts  0.8 us

profile of v6, /device:TPU:0, one launch (start us, length us, event | category | flops | bytes accessed | tf_op | source)
XLA Modules:
  0.0 20.8 jit_solution(8536388114951312278)
XLA Ops:
  0.0 19.9 %shard_map.109 = bf16[2,128,1024]{2,1,0:T(8,128)(2,1)S(1)} custom-call(bf16[8,8]{1,0:T(8,128)(2,1)} %tap_hbm.1, f32[1024,128]{1,0:T(8,128)} %rec_hbm.1, s32[64,1024]{1,0:T(8,128)} %mask_hbm.1, s32[128,128]{1,0:T(8,128)} %delay_hbm.1, s32[128,128]{1,0:T(8,128)} %index_hbm.1, bf16[768,256]{1,0:T(8,128)(2,1)} %constant.12.clone.mix_hbm, ...), custom_call_target="tpu_custom_call" | custom-call | tf_op jit(solution)/shard_map/pallas_call | solution.py:692
  20.0 0.8 %copy.13 = bf16[2,128,1024]{2,1,0:T(8,128)(2,1)} copy(bf16[2,128,1024]{2,1,0:T(8,128)(2,1)S(1)} %shard_map.109) | data formatting | bytes 1048576

commit v7 on v4

--- a/solution.py
+++ b/solution.py
@@ -648,11 +648,13 @@
     ext[2, middle:end, :STRIDE] = swapped_rim[:, :STRIDE]
     for side in range(2):
         put_edge(side, 1)
-    shift_rows(2, 0, half_len + EDGE)
+    shift_rows(2, 0, half_len - TILE + 2 * EDGE)
+    shift_rows(2, half_len - EDGE, 2 * EDGE)
     cut = 2 * EDGE
     many = half_len - TILE - EDGE
     firsts, lasts = ((EDGE, many),), ((EDGE + many, core - many),)
     more = dot_f32(operand([(1, outside), (2, outside), (2, firsts)]), weights[1])
+    shift_rows(2, half_len - TILE + 2 * EDGE, TILE - 3 * EDGE)
     keep_sums(0, around[:cut] + more[:cut], outside)
     keep_sums(1, around[cut:] + more[cut : 2 * cut], outside)
     keep_sums(1, partial[:many] + more[2 * cut :], firsts)

time: 20.9 us -> 20.9 us (level)
  no operation moved by 1% of the time
where the time goes in v7:
time: 20.9 us; the launch traced here: 20.8 us
  Pallas kernels  20 us (96%)
  local copies, waits for them, and re-layouts  0.8 us (4%)
    pallas_call x1, Pallas kernels, fused_body(): pl.pallas_call(functools.partial(fused, devices, blocks), out_shape=pltpu...  20 us
    unnamed x1, local copies, waits for them, and re-layouts  0.8 us

profile of v7, /device:TPU:0, one launch (start us, length us, event | category | flops | bytes accessed | tf_op | source)
XLA Modules:
  0.0 20.8 jit_solution(3799600726800300819)
XLA Ops:
  0.0 20.0 %shard_map.109 = bf16[2,128,1024]{2,1,0:T(8,128)(2,1)S(1)} custom-call(bf16[8,8]{1,0:T(8,128)(2,1)} %tap_hbm.1, f32[1024,128]{1,0:T(8,128)} %rec_hbm.1, s32[64,1024]{1,0:T(8,128)} %mask_hbm.1, s32[128,128]{1,0:T(8,128)} %delay_hbm.1, s32[128,128]{1,0:T(8,128)} %index_hbm.1, bf16[768,256]{1,0:T(8,128)(2,1)} %constant.12.clone.mix_hbm, ...), custom_call_target="tpu_custom_call" | custom-call | tf_op jit(solution)/shard_map/pallas_call | solution.py:695
  20.0 0.8 %copy.13 = bf16[2,128,1024]{2,1,0:T(8,128)(2,1)} copy(bf16[2,128,1024]{2,1,0:T(8,128)(2,1)S(1)} %shard_map.109) | data formatting | bytes 1048576
